TPU v7x, 32 devices: a whole 2x2x4 slice. The times are simulated.
32 devices in a mesh: front: 4 (over x, core), row: 2 (over y), col: 4 (over z).
Axes of the slice: x: 2, y: 2, z: 4, core: 2. Of those that a mesh axis runs over, the one named last changes fastest.
Arguments:
- parent_entries: float32 [12288, 12288], P('row', ('front', 'col')), as said below
- child_update: float32 [4, 8192, 8192], P('front', 'row', 'col'), as said below
- child_map: int32 [4, 64], replicated, may hold values from 0 to 95, as said below
- child_mask: int32 [4, 64, 64], P('front'), may hold values from 0 to 1, as said below
Outputs:
- schur: float32 [12288, 12288], P('row', ('front', 'col'))
- panel: float32 [12288, 512], P('row')
Inputs may be any that keep to these rules, and one draw needn't show every extreme that they name: `child_update`: each child's update matrix is symmetric. `parent_entries`: Symmetric. `child_mask`: symmetric in its last two dimensions, ones on the diagonal. Distinct within each child. With v = j mod (16), e = v mod (8), r = (v mod 16) div (8), k = (v div 16) * 8 + e and g = r * 8 + k div (1), child_map[f, j] div (6) equals g.
All inputs are finite; a program needn't handle non-finite values.
Results may differ from a plain program's by a relative error of at most 0.000071.
Values sent between devices are 32-bit elements; how exact they have to be, the bound alone decides.
A program may use at most 256 MiB of HBM per device.

v0:
```python
import jax
import jax.numpy as jnp
from jax import lax
from jax.sharding import PartitionSpec as P

W = 512
BLK = 128


def broadcast(block, axis, holder):
    block = jnp.where(lax.axis_index(axis) == holder, block, jnp.zeros_like(block))
    return lax.psum(block, axis)


def lookup_table(table, wanted, length):
    positions = jnp.arange(length, dtype=jnp.int32)
    return jnp.sum(jnp.where(wanted[..., None] == positions, table, 0), axis=-1)


def body(parent_entries, child_update, child_map, child_mask):
    grid_rows = lax.axis_size("row")
    grid_cols = lax.axis_size("col")
    groups = lax.axis_size(("front", "col"))
    row_index = lax.axis_index("row")
    column_index = lax.axis_index("col")
    group_index = lax.axis_index(("front", "col"))
    local = child_update[0]
    row_blocks = local.shape[0] // BLK
    column_blocks = local.shape[1] // BLK
    total_blocks = child_map.shape[1]
    fronts_count = child_map.shape[0]
    span = min(row_blocks, column_blocks)
    share = span // grid_rows
    per_group = column_blocks // groups
    group_ratio = groups // grid_rows
    front_rows = parent_entries.shape[0]
    front_cols = parent_entries.shape[1]
    parent_row_blocks = front_rows // BLK
    parent_col_blocks = front_cols // BLK
    window = lax.dynamic_slice(
        child_mask[0],
        (row_index * row_blocks, column_index * column_blocks),
        (row_blocks, column_blocks),
    )
    window = window.astype(jnp.float32)
    tiles = local.reshape(row_blocks, BLK, column_blocks, BLK) * window[:, None, :, None]
    tiles = tiles.reshape(
        row_blocks // span, grid_rows, share, BLK, column_blocks // span, grid_rows, share, BLK
    )
    tiles = tiles.transpose(1, 0, 2, 3, 5, 4, 6, 7)
    tiles = tiles.reshape(grid_rows, row_blocks // grid_rows, BLK, groups, per_group, BLK)
    moved = lax.all_to_all(tiles, "row", split_axis=0, concat_axis=0, tiled=True)
    arrived = lax.all_to_all(moved, ("front", "col"), split_axis=3, concat_axis=3, tiled=True)
    sources = jnp.arange(groups, dtype=jnp.int32)
    source_front = sources // grid_cols
    source_column = sources % grid_cols
    picker = source_front[:, None] == jnp.arange(fronts_count, dtype=jnp.int32)[None, :]
    map_rows = jnp.sum(jnp.where(picker[:, :, None], child_map[None, :, :], 0), axis=1)
    from_rows = jnp.arange(grid_rows, dtype=jnp.int32)
    steps_rows = jnp.arange(row_blocks // grid_rows, dtype=jnp.int32)
    child_rows = (
        from_rows[:, None] * row_blocks
        + steps_rows[None, :] // share * span
        + row_index * share
        + steps_rows[None, :] % share
    )
    row_slots = (
        lookup_table(map_rows[:, None, None, :], child_rows[None, :, :], total_blocks)
        - row_index * parent_row_blocks
    )
    steps_cols = jnp.arange(per_group, dtype=jnp.int32)
    ranked = group_index % group_ratio * per_group + steps_cols
    within = ranked // share * span + group_index // group_ratio * share + ranked % share
    child_cols = source_column[:, None] * column_blocks + within[None, :]
    col_slots = (
        lookup_table(map_rows[:, None, :], child_cols, total_blocks)
        - group_index * parent_col_blocks
    )
    row_hits = (
        row_slots[None] == jnp.arange(parent_row_blocks, dtype=jnp.int32)[:, None, None, None]
    )
    col_hits = col_slots[None] == jnp.arange(parent_col_blocks, dtype=jnp.int32)[:, None, None]
    placement = (row_hits[:, None, :, :, :, None] & col_hits[None, :, :, None, None, :]).astype(
        jnp.float32
    )
    assembled = jnp.einsum(
        "absrtw,rtxswy->axby", placement, arrived, precision=lax.Precision.HIGHEST
    )
    front = parent_entries + assembled.reshape(front_rows, front_cols)
    corner = broadcast(front[:W, :W], "row", 0)
    factor = jnp.linalg.cholesky(corner)
    solved = jax.scipy.linalg.solve_triangular(factor, front[:, :W].T, lower=True).T
    panel = broadcast(solved, ("front", "col"), 0)
    piece = lax.dynamic_slice_in_dim(panel, group_index % group_ratio * front_cols, front_cols, 0)
    across = broadcast(piece, "row", group_index // group_ratio)
    schur = front - jnp.dot(panel, across.T, precision=lax.Precision.HIGHEST)
    global_rows = row_index * front_rows + jnp.arange(front_rows, dtype=jnp.int32)
    global_cols = group_index * front_cols + jnp.arange(front_cols, dtype=jnp.int32)
    keep = (global_rows[:, None] >= W) & (global_cols[None, :] >= W)
    return (jnp.where(keep, schur, 0.0), panel)


def solution(mesh):
    placed = (P("row", ("front", "col")), P("front", "row", "col"), P(), P("front", None, None))
    return jax.shard_map(
        body,
        mesh=mesh,
        in_specs=placed,
        out_specs=(P("row", ("front", "col")), P("row", None)),
        check_vma=False,
    )
```

profile of v0, /device:TPU:12, one launch (start us, length us, event | category | flops | bytes accessed | tf_op | source)
XLA Modules:
  0.0 1818.6 jit_solution(11675411458818334902)
XLA Ops:
  7.2 0.7 copy-done
  8.2 27.5 %copy.105 = f32[512,8,16,128]{3,2,1,0:T(8,128)} copy(f32[512,8,16,128]{3,1,2,0:T(8,128)} %bitcast.91) | data formatting | bytes 67108864
  35.7 28.3 %copy_multiply_fusion = f32[2,2,8,128,1,2,8,128]{7,2,0,6,5,3,1,4:T(8,128)S(1)} fusion(f32[2,2,8,128,1,2,8,128]{7,6,5,3,2,1,0,4:T(8,128)} %bitcast.89, f32[2,2,8,2,8]{2,0,4,3,1:T(2,128)S(1)} %copy.79), kind=kLoop, calls=%fused_computation.5 | loop fusion | flops 8388608 | bytes 67110912 | tf_op jit(solution)/shard_map/mul | solution.py:46
  64.1 369.1 %all_to_all.10 = f32[2,16,128,16,1,128]{5,1,3,2,4,0:T(8,128)} all-to-all(f32[2,16,128,16,1,128]{5,1,3,2,4,0:T(8,128)S(1)} %bitcast.88), channel_id=1, replica_groups=mesh['front'=4,'row'=2,'col'=4] {'row'}, dimensions={0} | all-to-all | bytes 67108864 | tf_op jit(solution)/shard_map/all_to_all | solution.py:52
  433.1 24.2 %copy.81 = f32[2,16,128,16,1,128]{5,1,0,2,4,3:T(8,128)} copy(f32[2,16,128,16,1,128]{5,1,3,2,4,0:T(8,128)} %all_to_all.10) | data formatting | bytes 67108864 | tf_op jit(solution)/shard_map/all_to_all | solution.py:52
  457.3 6.3 all-to-all-start.1
  463.6 0.2 all-reduce.5.cloned.1.call-start
  464.0 18.7 %copy.85 = f32[6144,768]{0,1:T(8,128)} copy(f32[6144,768]{1,0:T(8,128)} %param.4) | data formatting | bytes 37748736 | tf_op args[0]
  482.8 0.2 select_reduce_fusion.6
  483.1 0.7 select_reduce_fusion
  483.8 0.1 iota_compare_fusion.1
  483.9 699.4 %all-to-all-done.1 = f32[2,16,128,16,1,128]{5,1,0,2,4,3:T(8,128)} async-done(((f32[2,16,128,16,1,128]{5,1,0,2,4,3:T(8,128)}), f32[2,16,128,16,1,128]{5,1,0,2,4,3:T(8,128)}, u32[]{:S(2)}, u32[]{:S(2)}) %all-to-all-start.1) | async-done | bytes 33554464 | tf_op jit(solution)/shard_map/all_to_all | solution.py:53
  1183.4 27.7 %fusion.10 = f32[48,128,6,128]{3,0,2,1:T(8,128)} fusion(f32[2,16,128,16,1,128]{5,1,0,2,4,3:T(8,128)} %all-to-all-done.1, pred[6,16]{1,0:T(8,128)(4,1)S(1)} %iota_compare_fusion.6, pred[48,16,2,16]{0,3,1,2:T(8,128)(4,1)S(1)} %iota_compare_fusion.1), kind=kOutput, calls=%fused_computation.17 | convolution fusion | flops 28991176704 | bytes 52453472 | tf_op jit(solution)/shard_map/absrtw,rtxswy->axby/dot_general | solution.py:86
  1211.1 18.9 %copy.84 = f32[48,128,6,128]{1,0,3,2:T(8,128)} copy(f32[48,128,6,128]{3,0,2,1:T(8,128)} %fusion.10) | data formatting | bytes 37748736 | tf_op jit(solution)/shard_map/absrtw,rtxswy->axby/transpose | solution.py:86
  1230.0 15.6 bitcast_add_fusion
  1245.5 6.8 copy-done.2
  1252.4 1.1 slice_select_fusion
  1253.5 0.4 all-reduce.7.cloned.1.call-start
  1254.0 10.8 slice_bitcast_fusion
  1264.8 30.3 %all-reduce.5.cloned.1.call-done = f32[512,512]{0,1:T(8,128)} async-done(((f32[512,512]{0,1:T(8,128)}), f32[512,512]{0,1:T(8,128)}) %all-reduce.5.cloned.1.call-update) | async-done | bytes 1048592 | tf_op jit(solution)/shard_map/psum | solution.py:12
  1295.2 1.6 copy.86
  1296.7 1.4 fusion.23
  1298.2 11.7 cholesky.103
  1309.9 9.8 custom-call.31
  1319.7 0.3 fusion.29
  1320.1 0.3 convolution_subtract_fusion.2
  1320.4 11.7 cholesky.215
  1332.3 0.1 copy.88
  1332.5 10.0 custom-call.32
  1342.6 0.3 convolution_dynamic-update-slice_fusion
  1343.0 0.6 convolution_subtract_fusion.3
  1343.6 11.7 cholesky.236
  1355.4 9.8 custom-call.33
  1365.2 0.3 convolution_dynamic-update-slice_fusion.1
  1365.5 0.5 convolution_subtract_fusion.4
  1366.0 12.1 cholesky.253
  1378.3 0.6 compare_reduce_fusion.2
  1378.9 0.7 compare_reduce_fusion.3
  1379.6 0.7 compare_reduce_fusion.1
  1380.3 0.7 compare_reduce_fusion
  1383.7 8.6 while.1
  1383.7 0.6 fusion.57
  1384.3 1.3 dynamic-slice.8
  1385.9 0.6 fusion.57
  1386.5 1.3 dynamic-slice.8
  1388.0 0.6 fusion.57
  1388.6 1.3 dynamic-slice.8
  1390.2 0.6 fusion.57
  1390.8 1.3 dynamic-slice.8
  1392.3 39.3 %custom-call.34 = f32[4,128,128]{1,2,0:T(8,128)S(1)} custom-call(f32[4,128,128]{2,1,0:T(8,128)S(1)} %get-tuple-element.9), custom_call_target="InvertDiagBlocksLowerTriangular" | custom-call | tf_op jit(solution)/shard_map/jit(_solve_triangular)/triangular_solve | solution.py:92
  1431.6 4.7 fusion.19
  1436.3 4.9 convolution_subtract_fusion
  1441.2 2.9 fusion.37
  1444.1 5.8 convolution_subtract_fusion.1
  1449.9 3.0 fusion.35
  1453.0 8.1 fusion.13
  1461.1 2.8 fusion.34
  1463.9 5.2 fusion.3
  1469.2 233.8 %all-reduce.7.cloned.1.call-done = f32[6144,512]{0,1:T(8,128)} async-done(((f32[6144,512]{0,1:T(8,128)}), f32[6144,512]{0,1:T(8,128)}) %all-reduce.7.cloned.1.call-update) | async-done | bytes 12582928 | tf_op jit(solution)/shard_map/psum | solution.py:12
  1703.0 2.7 dynamic-slice_select_fusion
  1705.7 12.7 copy.97
  1718.4 38.1 %all-reduce.9.cloned.1.call-done = f32[768,512]{0,1:T(8,128)} async-done(((f32[768,512]{0,1:T(8,128)}), f32[768,512]{0,1:T(8,128)}) %all-reduce.9.cloned.1.call-update) | async-done | bytes 1572880 | tf_op jit(solution)/shard_map/psum | solution.py:12
  1756.4 36.7 %subtract_select_fusion = f32[6144,768]{0,1:T(8,128)} fusion(f32[6144,768]{0,1:T(8,128)} %copy-done.2, pred[6144]{0:T(1024)(128)(4,1)S(1)} %add_compare_fusion, pred[768]{0:T(1024)(128)(4,1)S(1)} %add_compare_fusion.1, f32[6144,512]{0,1:T(8,128)} %all-reduce.7.cloned.1.call-done, f32[768,512]{0,1:T(8,128)} %all-reduce.9.cloned.1.call-done), kind=kOutput, calls=%fused_computation.7 | convolution fusion | flops 29005185024 | bytes 51911424 | tf_op jit(solution)/shard_map/dot_general | solution.py:96
  1793.2 18.6 %copy.96 = f32[6144,768]{1,0:T(8,128)} copy(f32[6144,768]{0,1:T(8,128)} %subtract_select_fusion) | data formatting | bytes 37748736
  (59 shorter events, 2.2 us)
Async XLA Ops:
  7.2 0.8 copy-start
  457.3 726.0 %all-to-all-start.1 = ((f32[2,16,128,16,1,128]{5,1,0,2,4,3:T(8,128)}), f32[2,16,128,16,1,128]{5,1,0,2,4,3:T(8,128)}, u32[]{:S(2)}, u32[]{:S(2)}) async-start(f32[2,16,128,16,1,128]{5,1,0,2,4,3:T(8,128)} %copy.81), calls=%async_computation.1 | async-start | bytes 67108864 | tf_op jit(solution)/shard_map/all_to_all | solution.py:53
  463.6 831.5 %all-reduce.5.cloned.1.call-start = ((), (), s32[]{:S(2)}) async-start(), calls=%async_computation.2 | async-start | bytes 2097152 | tf_op jit(solution)/shard_map/psum | solution.py:12
  464.0 18.7 %copy-start.3 = (s32[4,64]{1,0:T(4,128)S(1)}, s32[4,64]{1,0:T(4,128)}, u32[]{:S(2)}) copy-start(s32[4,64]{1,0:T(4,128)} %param.6) | copy-start | bytes 3076
  1245.5 6.9 copy-start.2
  1253.5 449.5 %all-reduce.7.cloned.1.call-start = ((), (), s32[]{:S(2)}) async-start(), calls=%async_computation.3 | async-start | bytes 25165824 | tf_op jit(solution)/shard_map/psum | solution.py:12
  1469.2 287.3 %all-reduce.9.cloned.1.call-start = ((), (), s32[]{:S(2)}) async-start(), calls=%async_computation.4 | async-start | bytes 3145728 | tf_op jit(solution)/shard_map/psum | solution.py:12
  1793.2 18.6 %copy-start.1 = (s32[1,64,64]{2,1,0:T(8,128)S(1)}, s32[1,64,64]{2,1,0:T(8,128)}, u32[]{:S(2)}) copy-start(s32[1,64,64]{2,1,0:T(8,128)} %param.7) | copy-start | bytes 49156
Sparse Core Ops, SparseCore 0:
  1253.6 41.4 all-reduce.4
  1469.3 233.6 all-reduce.6
  1705.8 50.5 all-reduce.8
where the time goes:
time: 1830 us; the launch traced here: 1820 us
  waiting for transfers between devices  1000 us (55%)
  blocking collectives  369 us (20%)
  other arithmetic  175 us (10%)
  local copies, waits for them, and re-layouts  150 us (8%)
  matrix products  99.1 us (5%)
    all_to_all x1, waiting for transfers between devices, body(): lax.all_to_all(moved, ('front', 'col'), split_axis=3, concat_axis=3, tile...  699 us
    all_to_all x1, blocking collectives, body(): lax.all_to_all(tiles, 'row', split_axis=0, concat_axis=0, tiled=True)  369 us
    psum x3, waiting for transfers between devices, broadcast(): return lax.psum(block, axis)  302 us
    unnamed x13, local copies, waits for them, and re-layouts  85.2 us
    another operation x15, other arithmetic, body(): factor = jnp.linalg.cholesky(corner)  79.7 us
    another operation x3, other arithmetic, body(): jax.scipy.linalg.solve_triangular(factor, front[:, :W].T, lower=True)  39.4 us
    dot_general x1, matrix products, body(): schur = front - jnp.dot(panel, across.T, precision=lax.Precision.HIGHEST)  36.7 us
  transfers between devices with their start and end apart: 4, of which 4 were waited for; matrix products, arithmetic and copies ran while one was open for 2% of the time, Pallas kernels for 0%

commit v1 on v0

v1 whole, which is shorter than its diff:
```python
import functools

import jax
import jax.numpy as jnp
from jax import lax
from jax.experimental import pallas as pl
from jax.experimental.pallas import tpu as pltpu
from jax.sharding import PartitionSpec as P

W = 512
BLK = 128
MESH = pl.DeviceIdType.MESH
HIGHEST = lax.Precision.HIGHEST


class Sizes:
    def __init__(self, mesh, child_rows, child_cols):
        self.fronts = mesh.shape["front"]
        self.rows = mesh.shape["row"]
        self.cols = mesh.shape["col"]
        self.groups = self.fronts * self.cols
        self.row_blocks = child_rows // BLK
        self.period = child_cols // BLK
        self.span = min(self.row_blocks, self.period)
        self.share = self.span // self.rows
        self.ratio = self.groups // self.rows
        self.parts = self.period // self.span
        self.units = self.row_blocks // self.span
        self.holds = max(1, self.row_blocks // self.period)


def rank(place, target, cols):
    away = jnp.abs(place - target)
    low = jnp.where(place > target, 1, 0)
    high = jnp.where(place < target, 1, 0)
    return 2 * away + jnp.where(target * 2 < cols, low, high)


def exchange_kernel(s, lead, child_ref, mask_ref, direct_ref, turned_ref, *rest):
    if lead:
        masks_ref, send_sem, recv_sem, mask_sem = rest
    else:
        send_sem, recv_sem = rest
    f = lax.axis_index("front")
    r = lax.axis_index("row")
    z = lax.axis_index("col")
    devices = s.groups * s.rows
    me = (f * s.rows + r) * s.cols + z
    targets = s.groups if lead else devices
    height = BLK if lead else s.share * BLK
    parts = 1 if lead else s.parts

    def place(step):
        other = lax.rem(me + step, devices)
        return other // (s.rows * s.cols), other // s.cols % s.rows, other % s.cols

    barrier = pltpu.get_barrier_semaphore()

    @pl.loop(1, devices)
    def greet(step):
        tf, tr, tz = place(step)
        pl.semaphore_signal(barrier, inc=1, device_id=(tf, tr, tz), device_id_type=MESH)

    pl.semaphore_wait(barrier, devices - 1)

    def lead_place(step):
        spot = f * s.cols + z
        other = lax.rem(spot + step, s.groups)
        return other // s.cols, 0, other % s.cols

    def visit(step, act):
        tf, tr, tz = lead_place(step) if lead else place(step)
        group = tf * s.cols + tz
        k = group % s.ratio
        v = k // s.share * s.span + group // s.ratio * s.share + k % s.share
        own = (tf == f) & (tr == r) & (tz == z)
        near = rank(z, tz, s.cols)
        for t in range(s.units):
            u = r * s.units + t
            a, h = u // s.parts, u % s.parts
            chosen = near <= rank(a, tz, s.cols)
            if lead:
                chosen = chosen & (h == 0)
            source = child_ref.at[
                pl.ds(pl.multiple_of((t * s.span + tr * s.share) * BLK, BLK), height),
                pl.ds(pl.multiple_of(v * BLK, BLK), BLK),
            ]
            target = direct_ref.at[f, z, a, h]
            act(chosen, own, source, target, (tf, tr, tz), step, t, (z, a, h))
        for t in range(s.holds):
            c = r * s.row_blocks // s.period + t
            line = s.period * c + v - r * s.row_blocks
            held = (line >= 0) & (line < s.row_blocks)
            chosen = held & (near < rank(c, tz, s.cols))
            line = jnp.clip(line, 0, s.row_blocks - 1)
            for h in range(parts):
                source = child_ref.at[
                    pl.ds(pl.multiple_of(line * BLK, BLK), BLK),
                    pl.ds(pl.multiple_of((h * s.span + tr * s.share) * BLK, BLK), height),
                ]
                target = turned_ref.at[f, c, z, h]
                number = s.units + t * parts + h
                act(chosen, own, source, target, (tf, tr, tz), step, number, (c, z, h))

    def slot_of(c, a, h):
        return ((f * s.cols + c) * s.cols + a) * parts + h

    def start(chosen, own, source, target, where, step, number, unit):
        recv = recv_sem.at[slot_of(*unit)]

        @pl.when(chosen & own)
        def _():
            pltpu.make_async_copy(source, target, recv).start()

        @pl.when(chosen & jnp.logical_not(own))
        def _():
            pltpu.make_async_remote_copy(
                src_ref=source,
                dst_ref=target,
                send_sem=send_sem.at[step, number],
                recv_sem=recv,
                device_id=where,
                device_id_type=MESH,
            ).start()

    def finish(chosen, own, source, target, where, step, number, unit):
        @pl.when(chosen & jnp.logical_not(own))
        def _():
            pltpu.make_async_copy(source, target, send_sem.at[step, number]).wait()

    @pl.loop(0, targets)
    def send(step):
        visit(step, start)

    if lead:
        def mask_copy(hop):
            return pltpu.make_async_remote_copy(
                src_ref=mask_ref.at[0],
                dst_ref=masks_ref.at[f],
                send_sem=mask_sem.at[0, hop],
                recv_sem=mask_sem.at[1, hop],
                device_id=(lax.rem(f + hop, s.fronts), r, z),
                device_id_type=MESH,
            )

        for hop in range(1, s.fronts):
            mask_copy(hop).start()
        own_mask = pltpu.make_async_copy(mask_ref.at[0], masks_ref.at[f], mask_sem.at[0, 0])
        own_mask.start()
        own_mask.wait()
        for hop in range(1, s.fronts):
            mask_copy(hop).wait()

    def arrive():
        @pl.loop(0, s.fronts * s.cols * s.cols * parts)
        def wait(slot):
            first = direct_ref.at[0, 0, 0, 0]
            pltpu.make_async_copy(first, first, recv_sem.at[slot]).wait()

    if lead:
        pl.when(r == 0)(arrive)
    else:
        arrive()

    @pl.loop(0, targets)
    def drain(step):
        visit(step, finish)


def exchange(s, lead, child, mask):
    parts = 1 if lead else s.parts
    height = BLK if lead else s.share * BLK
    targets = s.groups if lead else s.groups * s.rows
    shapes = [
        jax.ShapeDtypeStruct((s.fronts, s.cols, s.cols, parts, height, BLK), jnp.float32),
        jax.ShapeDtypeStruct((s.fronts, s.cols, s.cols, parts, BLK, height), jnp.float32),
    ]
    scratch = [
        pltpu.SemaphoreType.DMA((targets, s.units + s.holds * parts)),
        pltpu.SemaphoreType.DMA((s.fronts * s.cols * s.cols * parts,)),
    ]
    if lead:
        shapes.append(jax.ShapeDtypeStruct((s.fronts,) + mask.shape[1:], jnp.int32))
        scratch.append(pltpu.SemaphoreType.DMA((2, s.fronts)))
    return pl.pallas_call(
        functools.partial(exchange_kernel, s, lead),
        out_shape=shapes,
        in_specs=[pl.BlockSpec(memory_space=pl.ANY)] * 2,
        out_specs=[pl.BlockSpec(memory_space=pl.ANY)] * len(shapes),
        scratch_shapes=scratch,
        compiler_params=pltpu.CompilerParams(
            collective_id=0 if lead else 1, has_side_effects=True
        ),
        name="lead_exchange" if lead else "exchange",
    )(child, mask)


def assemble(s, table_ref, chunk, parent_ref, direct_ref, turned_ref, front_ref, slots):
    @pl.loop(0, slots * slots)
    def block(spot):
        i, j = spot // slots, spot % slots
        rows = pl.ds(pl.multiple_of(i * BLK, BLK), BLK)
        cols = pl.ds(pl.multiple_of(j * BLK, BLK), BLK)
        front_ref[rows, cols] = parent_ref[rows, cols]
        for f in range(s.fronts):
            code = table_ref[((chunk * slots + i) * slots + j) * s.fronts + f]
            unit = jnp.maximum(code - 1, 0) // 2
            c, a = unit // s.cols, unit % s.cols

            @pl.when((code > 0) & (code % 2 == 1))
            def _():
                front_ref[rows, cols] += direct_ref[f, c, a, 0]

            @pl.when((code > 0) & (code % 2 == 0))
            def _():
                front_ref[rows, cols] += turned_ref[f, c, a, 0].T


def lead_kernel(s, slots, table_ref, parent_ref, direct_ref, turned_ref, front_ref):
    assemble(s, table_ref, 0, parent_ref, direct_ref, turned_ref, front_ref, slots)


def assemble_lead(s, slots, table, parent, direct, turned):
    side = slots * BLK
    blocks = (s.fronts, s.cols, s.cols, 1, BLK, BLK)
    return pl.pallas_call(
        functools.partial(lead_kernel, s, slots),
        grid_spec=pltpu.PrefetchScalarGridSpec(
            num_scalar_prefetch=1,
            grid=(1,),
            in_specs=[
                pl.BlockSpec((side, side), lambda k, t: (0, 0)),
                pl.BlockSpec(blocks, lambda k, t: (0,) * 6),
                pl.BlockSpec(blocks, lambda k, t: (0,) * 6),
            ],
            out_specs=pl.BlockSpec((side, side), lambda k, t: (0, 0)),
        ),
        out_shape=jax.ShapeDtypeStruct((side, side), jnp.float32),
        compiler_params=pltpu.CompilerParams(vmem_limit_bytes=48 << 20),
        name="assemble_lead",
    )(table, parent, direct, turned)


def dot(x, y):
    return lax.dot_general(
        x, y, (((1,), (0,)), ((), ())), precision=HIGHEST, preferred_element_type=jnp.float32
    )


def dot_turned(x, y):
    return lax.dot_general(
        x, y, (((1,), (1,)), ((), ())), precision=HIGHEST, preferred_element_type=jnp.float32
    )


def invert_kernel(corner_ref, right_ref, out_ref, work, lower, eliminate, gather):
    count = W // BLK
    work[...] = corner_ref[...]
    line = lax.broadcasted_iota(jnp.int32, (BLK, 1), 0)
    lane = lax.broadcasted_iota(jnp.int32, (BLK, BLK), 1)
    for b in range(count):
        here = slice(b * BLK, (b + 1) * BLK)
        eliminate[...] = work[here, here]
        gather[...] = jnp.where(line == lane, 1.0, 0.0)

        @pl.loop(0, BLK)
        def step(j):
            block = eliminate[...]
            pivot_row = eliminate[pl.ds(j, 1), :]
            identity_row = gather[pl.ds(j, 1), :]
            column = jnp.sum(jnp.where(lane == j, block, 0.0), axis=1, keepdims=True)
            pivot = jnp.sum(jnp.where(line == j, column, 0.0), axis=0, keepdims=True)
            root = lax.rsqrt(pivot)
            root = root * (1.5 - 0.5 * pivot * root * root)
            scale = jnp.where(line > j, column / pivot, 0.0)
            keep = jnp.where(line == j, root, 1.0)
            eliminate[...] = block - scale * pivot_row
            gather[...] = (gather[...] - scale * identity_row) * keep

        inverse = gather[...]
        if b + 1 < count:
            below = slice((b + 1) * BLK, W)
            panel = dot_turned(work[below, here], inverse)
            lower[below, here] = panel
            work[below, below] = work[below, below] - dot_turned(panel, panel)
        total = right_ref[here, :]
        if b:
            total = total - dot(lower[here, 0 : b * BLK], out_ref[0 : b * BLK, :])
        out_ref[here, :] = dot(inverse, total)


def solve(corner, right):
    return pl.pallas_call(
        invert_kernel,
        out_shape=jax.ShapeDtypeStruct(right.shape, jnp.float32),
        scratch_shapes=[
            pltpu.VMEM((W, W), jnp.float32),
            pltpu.VMEM((W, W), jnp.float32),
            pltpu.VMEM((BLK, BLK), jnp.float32),
            pltpu.VMEM((BLK, BLK), jnp.float32),
        ],
        compiler_params=pltpu.CompilerParams(vmem_limit_bytes=48 << 20),
        name="factor_and_solve",
    )(corner, right)


def schur_kernel(s, slots, table_ref, place_ref, parent_ref, direct_ref, turned_ref, across_ref, *rest):
    pieces = rest[: s.rows]
    schur_ref, panel_ref, front = rest[s.rows :]
    k = pl.program_id(0)
    assemble(s, table_ref, k, parent_ref, direct_ref, turned_ref, front, slots)
    part = slots * BLK // s.rows
    for n in range(s.rows):
        panel_ref[n * part : (n + 1) * part, :] = pieces[n][0]
    side = slots * BLK
    product = dot_turned(panel_ref[...], across_ref[...])
    rows = place_ref[0] + k * side + lax.broadcasted_iota(jnp.int32, (side, 1), 0)
    cols = place_ref[1] + lax.broadcasted_iota(jnp.int32, (1, side), 1)
    schur_ref[...] = jnp.where((rows >= W) & (cols >= W), front[...] - product, 0.0)


def assemble_schur(s, slots, table, place, parent, direct, turned, across, gathered):
    side = slots * BLK
    steps = parent.shape[0] // side
    part = side // s.rows
    blocks = (s.fronts, s.cols, s.cols, 1, BLK, BLK)
    return pl.pallas_call(
        functools.partial(schur_kernel, s, slots),
        grid_spec=pltpu.PrefetchScalarGridSpec(
            num_scalar_prefetch=2,
            grid=(steps,),
            in_specs=[
                pl.BlockSpec((side, side), lambda k, t, p: (k, 0)),
                pl.BlockSpec(blocks, lambda k, t, p: (0, 0, 0, k // s.share, k % s.share, 0)),
                pl.BlockSpec(blocks, lambda k, t, p: (0, 0, 0, k // s.share, 0, k % s.share)),
                pl.BlockSpec((side, W), lambda k, t, p: (0, 0)),
            ]
            + [
                pl.BlockSpec((1, part, W), functools.partial(lambda n, k, t, p: (n * s.ratio + k, 0, 0), n))
                for n in range(s.rows)
            ],
            out_specs=[
                pl.BlockSpec((side, side), lambda k, t, p: (k, 0)),
                pl.BlockSpec((side, W), lambda k, t, p: (k, 0)),
            ],
            scratch_shapes=[pltpu.VMEM((side, side), jnp.float32)],
        ),
        out_shape=[
            jax.ShapeDtypeStruct(parent.shape, jnp.float32),
            jax.ShapeDtypeStruct((parent.shape[0], W), jnp.float32),
        ],
        compiler_params=pltpu.CompilerParams(vmem_limit_bytes=56 << 20),
        name="assemble_schur",
    )(table, place, parent, direct, turned, across, *([gathered] * s.rows))


def body(mesh, parent_entries, child_update, child_map, child_mask):
    child = child_update[0]
    s = Sizes(mesh, *child.shape)
    row_index = lax.axis_index("row")
    column_index = lax.axis_index("col")
    group_index = lax.axis_index(("front", "col"))
    front_rows, front_cols = parent_entries.shape
    slots = front_cols // BLK

    lead_direct, lead_turned, masks = exchange(s, True, child, child_mask)

    def sources(first, count):
        places = first + jnp.arange(count, dtype=jnp.int32)
        return child_map[:, None, :] == places[None, :, None]

    on_rows = sources(row_index * (front_rows // BLK), front_rows // BLK)
    on_cols = sources(group_index * slots, slots)
    kept = jnp.einsum(
        "fap,fpq,fbq->abf",
        on_rows.astype(jnp.float32),
        masks.astype(jnp.float32),
        on_cols.astype(jnp.float32),
    )
    numbers = jnp.arange(child_map.shape[1], dtype=jnp.int32) // s.period
    row_unit = jnp.sum(jnp.where(on_rows, numbers, 0), axis=-1).T[:, None, :]
    col_unit = jnp.sum(jnp.where(on_cols, numbers, 0), axis=-1).T[None, :, :]
    straight = rank(col_unit, column_index, s.cols) <= rank(row_unit, column_index, s.cols)
    code = 1 + 2 * (col_unit * s.cols + row_unit) + jnp.where(straight, 0, 1)
    table = jnp.where(kept > 0.5, code, 0).astype(jnp.int32).reshape(-1)

    lead = assemble_lead(s, slots, table, parent_entries, lead_direct, lead_turned)[:W]
    corner = lax.psum(jnp.where(group_index == 0, lead[:, :W], 0.0), ("front", "col"))
    solved = solve(corner, lead)
    piece = solved.T
    across = piece
    for r in range(1, s.rows):
        moved = lax.ppermute(piece, "row", [(0, r)])
        across = jnp.where(row_index == r, moved, across)

    part = front_cols // s.rows
    mine = lax.dynamic_slice_in_dim(across, row_index * part, part, 0)
    slot = mine
    owner = group_index // s.ratio
    for shift in range(1, s.rows):
        wanted = lax.rem(row_index + shift, s.rows)
        pairs = []
        for r in range(s.rows):
            for k in range(s.ratio):
                a, b = s.ratio * r + k, s.ratio * ((r + shift) % s.rows) + k
                index = [(g // s.cols * s.rows + r) * s.cols + g % s.cols for g in (a, b)]
                pairs.append(tuple(index))
        sent = lax.dynamic_slice_in_dim(across, wanted * part, part, 0)
        got = lax.ppermute(sent, ("front", "row", "col"), pairs)
        slot = jnp.where(owner == wanted, got, slot)
    gathered = lax.all_gather(slot, ("front", "col"))

    direct, turned = exchange(s, False, child, child_mask)
    place = jnp.stack([row_index * front_rows, group_index * front_cols]).astype(jnp.int32)
    return tuple(
        assemble_schur(
            s, slots, table, place, parent_entries, direct, turned, across, gathered
        )
    )


def solution(mesh):
    placed = (P("row", ("front", "col")), P("front", "row", "col"), P(), P("front", None, None))
    return jax.shard_map(
        functools.partial(body, mesh),
        mesh=mesh,
        in_specs=placed,
        out_specs=(P("row", ("front", "col")), P("row", None)),
        check_vma=False,
    )
```

time: 1830 us -> 1260 us (0.69)
  Pallas kernels: 0 us -> 1090 us
  waiting for transfers between devices: 1000 us -> 144 us
  blocking collectives: 369 us -> 0 us
  other arithmetic: 175 us -> 6.42 us
  local copies, waits for them, and re-layouts: 150 us -> 4.89 us
  matrix products: 99.1 us -> 1.16 us
    pallas_call x0 -> x5, Pallas kernels: none -> 1090 us  [the longest x2 916 us: exchange(): pl.pallas_call(functools.partial(exchange_kernel, s, lead), out_shape=sha...]
    all_to_all x1 -> x0, waiting for transfers between devices: 699 us -> none  [body(): lax.all_to_all(moved, ('front', 'col'), split_axis=3, concat_axis=3, tile...]
    all_to_all x1 -> x0, blocking collectives: 369 us -> none  [body(): lax.all_to_all(tiles, 'row', split_axis=0, concat_axis=0, tiled=True)]
    psum x3 -> x1, waiting for transfers between devices: 302 us -> 92.4 us  [body(): lax.psum(jnp.where(group_index == 0, lead[:, :W], 0.0), ('front', 'col'))]
    another operation x18 -> x1, other arithmetic: 119 us -> 0.67 us  [body(): jnp.stack([row_index * front_rows, group_index * front_cols])]
    unnamed x13 -> x10, local copies, waits for them, and re-layouts: 85.2 us -> 2.64 us
    dot_general x2 -> x1, matrix products: 64.5 us -> 1.16 us  [body(): jnp.einsum('fap,fpq,fbq->abf', on_rows.astype(jnp.float32), masks.astype(...]
    ppermute x0 -> x2, waiting for transfers between devices: none -> 51.8 us  [the longest x1 34.9 us: body(): moved = lax.ppermute(piece, 'row', [(0, r)])]
  transfers between devices with their start and end apart: 4 -> 4, of which waited for: 4 -> 3; matrix products, arithmetic and copies ran while one was open for 2% -> 0% of each run, Pallas kernels for 0% -> 67%
where the time goes in v1:
time: 1260 us
  Pallas kernels  1090 us (87%)
  waiting for transfers between devices  144 us (11%)
  between operations  14.3 us (1%)
    pallas_call x2, Pallas kernels, exchange(): pl.pallas_call(functools.partial(exchange_kernel, s, lead), out_shape=sha...  916 us
    psum x1, waiting for transfers between devices, body(): lax.psum(jnp.where(group_index == 0, lead[:, :W], 0.0), ('front', 'col'))  92.4 us
    pallas_call x1, Pallas kernels, assemble_schur(): pl.pallas_call(functools.partial(schur_kernel, s, slots), grid_spec=pltpu...  88.1 us
    pallas_call x1, Pallas kernels, solve(): pl.pallas_call(invert_kernel, out_shape=jax.ShapeDtypeStruct(right.shape,...  71.8 us
    ppermute x1, waiting for transfers between devices, body(): moved = lax.ppermute(piece, 'row', [(0, r)])  34.9 us
  transfers between devices with their start and end apart: 4, of which 3 were waited for; matrix products, arithmetic and copies ran while one was open for 0% of the time, Pallas kernels for 67%

profile of v1, /device:TPU:12, one launch (start us, length us, event | category | flops | bytes accessed | tf_op | source)
XLA Modules:
  0.0 1260.0 jit_solution(10315694584728913932)
XLA Ops:
  7.2 0.0 all-reduce.2.cloned.1.call-start
  7.3 0.9 fusion.15
  8.2 0.9 select_reduce_fusion
  9.1 0.1 copy.10
  9.2 0.1 copy.11
  9.3 0.0 copy-start.4
  9.3 73.9 %lead_exchange.1 = (f32[4,4,4,1,128,128]{5,4,3,2,1,0:T(8,128)}, f32[4,4,4,1,128,128]{5,4,3,2,1,0:T(8,128)}, s32[4,64,64]{2,1,0:T(8,128)}) custom-call(f32[4096,2048]{1,0:T(8,128)} %bitcast.16, s32[1,64,64]{2,1,0:T(8,128)} %mask_ref.3), custom_call_target="tpu_custom_call" | custom-call | tf_op jit(solution)/shard_map/lead_exchange/pallas_call | solution.py:185
  83.2 0.0 copy-done.4
  83.2 1.2 fusion.9
  84.4 0.2 copy.12
  84.5 0.1 reshape.39.table_ref
  84.7 0.0 copy-start.2
  84.7 10.6 assemble_lead.1
  95.3 0.0 copy-done.2
  95.3 1.1 slice_select_fusion
  96.4 0.0 all-reduce.2.cloned.1.call-update
  96.4 0.0 all-gather.3.cloned.1.call-start
  96.5 1.2 slice.10.right_ref
  97.7 92.4 %all-reduce.2.cloned.1.call-done.corner_ref = f32[512,512]{1,0:T(8,128)} async-done(((f32[512,512]{1,0:T(8,128)}), f32[512,512]{1,0:T(8,128)}) %all-reduce.2.cloned.1.call-update) | async-done | bytes 1048592 | tf_op jit(solution)/shard_map/psum | solution.py:388
  190.1 0.0 copy-start
  190.1 1.4 copy-done
  191.5 0.0 copy-start.1
  191.5 1.2 copy-done.1
  192.7 71.8 %factor_and_solve.1 = f32[512,768]{1,0:T(8,128)S(1)} custom-call(f32[512,512]{1,0:T(8,128)S(1)} %copy-done.1, f32[512,768]{1,0:T(8,128)S(1)} %copy-done), custom_call_target="tpu_custom_call" | custom-call | tf_op jit(solution)/shard_map/factor_and_solve/pallas_call | solution.py:293
  264.5 0.5 copy.13
  265.0 1.3 collective-permute-start
  266.3 34.9 %collective-permute-done = f32[768,512]{1,0:T(8,128)} collective-permute-done((f32[768,512]{1,0:T(8,128)S(1)}, f32[768,512]{1,0:T(8,128)}, u32[]{:S(2)}, u32[]{:S(2)}) %collective-permute-start) | collective-permute-done | bytes 1572896 | tf_op jit(solution)/shard_map/ppermute | solution.py:393
  301.2 1.8 broadcast_select_fusion.across_ref
  303.0 0.0 copy-start.3
  303.0 0.1 constant_dynamic-slice_fusion
  303.1 1.5 collective-permute-start.1
  304.6 16.8 %collective-permute-done.1 = f32[384,512]{1,0:T(8,128)S(1)} collective-permute-done((f32[384,512]{1,0:T(8,128)S(1)}, f32[384,512]{1,0:T(8,128)S(1)}, u32[]{:S(2)}, u32[]{:S(2)}) %collective-permute-start.1) | collective-permute-done | bytes 786464 | tf_op jit(solution)/shard_map/ppermute | solution.py:409
  321.4 1.0 dynamic-slice_select_fusion
  322.4 0.0 all-gather.3.cloned.1.call-update
  322.4 0.0 copy-done.3
  322.4 842.0 %exchange.1 = (f32[4,4,4,1,1024,128]{5,4,3,2,1,0:T(8,128)}, f32[4,4,4,1,128,1024]{5,4,3,2,1,0:T(8,128)}) custom-call(f32[4096,2048]{1,0:T(8,128)} %bitcast.17, s32[1,64,64]{2,1,0:T(8,128)} %mask_ref.3), custom_call_target="tpu_custom_call" | custom-call | tf_op jit(solution)/shard_map/exchange/pallas_call | solution.py:185
  1164.4 0.7 pad_add_fusion.place_ref
  1165.1 0.0 all-gather.3.cloned.1.call-done
  1165.1 88.1 %assemble_schur.1 = (f32[6144,768]{1,0:T(8,128)}, f32[6144,512]{1,0:T(8,128)}) custom-call(s32[1152]{0:T(1024)} %copy-done.2, s32[2]{0:T(128)} %pad_add_fusion.place_ref, f32[6144,768]{1,0:T(8,128)} %parent_ref.3, f32[4,4,4,1,1024,128]{5,4,3,2,1,0:T(8,128)} %get-tuple-element.8.direct_ref, f32[4,4,4,1,128,1024]{5,4,3,2,1,0:T(8,128)} %get-tuple-element.9.turned_ref, ...), custom_call_target="tpu_custom_call" | custom-call | tf_op jit(solution)/shard_map/assemble_schur/pallas_call | solution.py:327
  (5 shorter events, 0.0 us)
Async XLA Ops:
  7.2 182.9 %all-reduce.2.cloned.1.call-start = ((), (), s32[]{:S(2)}) async-start(), calls=%async_computation | async-start | bytes 2097152 | tf_op jit(solution)/shard_map/psum | solution.py:388
  9.3 73.9 %copy-start.4 = (s32[4,64]{1,0:T(4,128)S(1)}, s32[4,64]{1,0:T(4,128)}, u32[]{:S(2)}) copy-start(s32[4,64]{1,0:T(4,128)} %param.6) | copy-start | bytes 3076
  84.7 10.6 copy-start.2
  96.4 1068.6 %all-gather.3.cloned.1.call-start = ((), (), s32[]{:S(2)}) async-start(), calls=%async_computation.1 | async-start | bytes 13369344 | tf_op jit(solution)/shard_map/all_gather | solution.py:411
  190.1 1.4 copy-start
  191.5 1.2 copy-start.1
  265.0 36.2 %collective-permute-start = (f32[768,512]{1,0:T(8,128)S(1)}, f32[768,512]{1,0:T(8,128)}, u32[]{:S(2)}, u32[]{:S(2)}) collective-permute-start(f32[768,512]{1,0:T(8,128)S(1)} %bitcast.20), channel_id=1, source_target_pairs={{0,4},{1,5},{2,6},{3,7},{8,12},{9,13},{10,14},{11,15},{16,20},{17,... | collective-permute-start | bytes 4718600 | tf_op jit(solution)/shard_map/ppermute | solution.py:393
  303.0 19.5 %copy-start.3 = (f32[768,512]{1,0:T(8,128)}, f32[768,512]{1,0:T(8,128)S(1)}, u32[]{:S(2)}) copy-start(f32[768,512]{1,0:T(8,128)S(1)} %broadcast_select_fusion.across_ref) | copy-start | bytes 4718596
  303.1 18.3 %collective-permute-start.1 = (f32[384,512]{1,0:T(8,128)S(1)}, f32[384,512]{1,0:T(8,128)S(1)}, u32[]{:S(2)}, u32[]{:S(2)}) collective-permute-start(f32[384,512]{1,0:T(8,128)S(1)} %constant_dynamic-slice_fusion), channel_id=1, source_target_pairs={{0,16},{1,17},{2,18},{3,19},{8,24},{9,25},{10,26},{11,27},{20,4},{... | collective-permute-start | bytes 2359304 | tf_op jit(solution)/shard_map/ppermute | solution.py:409
Sparse Core Ops, SparseCore 0:
  96.6 93.4 all-reduce.1
  322.6 382.8 all-gather.2

commit v2 on v1

--- a/solution.py
+++ b/solution.py
@@ -45,14 +45,14 @@
     r = lax.axis_index("row")
     z = lax.axis_index("col")
     devices = s.groups * s.rows
-    me = (f * s.rows + r) * s.cols + z
     targets = s.groups if lead else devices
     height = BLK if lead else s.share * BLK
     parts = 1 if lead else s.parts
 
     def place(step):
-        other = lax.rem(me + step, devices)
-        return other // (s.rows * s.cols), other // s.cols % s.rows, other % s.cols
+        dz, turn = step % s.cols, step // s.cols
+        df, dr = (turn + dz) % s.fronts, (turn // s.fronts + dz) % s.rows
+        return lax.rem(f + df, s.fronts), lax.rem(r + dr, s.rows), lax.rem(z + dz, s.cols)
 
     barrier = pltpu.get_barrier_semaphore()
 
@@ -64,9 +64,9 @@
     pl.semaphore_wait(barrier, devices - 1)
 
     def lead_place(step):
-        spot = f * s.cols + z
-        other = lax.rem(spot + step, s.groups)
-        return other // s.cols, 0, other % s.cols
+        dz = step % s.cols
+        df = (step // s.cols + dz) % s.fronts
+        return lax.rem(f + df, s.fronts), 0, lax.rem(z + dz, s.cols)
 
     def visit(step, act):
         tf, tr, tz = lead_place(step) if lead else place(step)

time: 1260 us -> 1270 us (level)
  no operation moved by 1% of the time
where the time goes in v2:
time: 1270 us
  Pallas kernels  1090 us (86%)
  waiting for transfers between devices  144 us (11%)
  between operations  14.3 us (1%)
    pallas_call x2, Pallas kernels, exchange(): pl.pallas_call(functools.partial(exchange_kernel, s, lead), out_shape=sha...  924 us
    psum x1, waiting for transfers between devices, body(): lax.psum(jnp.where(group_index == 0, lead[:, :W], 0.0), ('front', 'col'))  92.4 us
    pallas_call x1, Pallas kernels, assemble_schur(): pl.pallas_call(functools.partial(schur_kernel, s, slots), grid_spec=pltpu...  87 us
    pallas_call x1, Pallas kernels, solve(): pl.pallas_call(invert_kernel, out_shape=jax.ShapeDtypeStruct(right.shape,...  71.8 us
    ppermute x1, waiting for transfers between devices, body(): moved = lax.ppermute(piece, 'row', [(0, r)])  34.9 us
  transfers between devices with their start and end apart: 4, of which 3 were waited for; matrix products, arithmetic and copies ran while one was open for 0% of the time, Pallas kernels for 67%

profile of v2, /device:TPU:12, one launch (start us, length us, event | category | flops | bytes accessed | tf_op | source)
XLA Modules:
  0.0 1267.1 jit_solution(6965199398210665572)
XLA Ops:
  7.2 0.0 all-reduce.2.cloned.1.call-start
  7.3 0.9 fusion.15
  8.2 0.9 select_reduce_fusion
  9.1 0.1 copy.10
  9.2 0.1 copy.11
  9.3 0.0 copy-start.4
  9.3 74.0 %lead_exchange.1 = (f32[4,4,4,1,128,128]{5,4,3,2,1,0:T(8,128)}, f32[4,4,4,1,128,128]{5,4,3,2,1,0:T(8,128)}, s32[4,64,64]{2,1,0:T(8,128)}) custom-call(f32[4096,2048]{1,0:T(8,128)} %bitcast.16, s32[1,64,64]{2,1,0:T(8,128)} %mask_ref.3), custom_call_target="tpu_custom_call" | custom-call | tf_op jit(solution)/shard_map/lead_exchange/pallas_call | solution.py:185
  83.3 0.0 copy-done.4
  83.3 1.2 fusion.9
  84.5 0.2 copy.12
  84.6 0.1 reshape.39.table_ref
  84.8 0.0 copy-start.2
  84.8 10.4 assemble_lead.1
  95.2 0.0 copy-done.2
  95.2 1.1 slice_select_fusion
  96.3 0.0 all-reduce.2.cloned.1.call-update
  96.4 0.0 all-gather.3.cloned.1.call-start
  96.4 1.2 slice.10.right_ref
  97.7 92.4 %all-reduce.2.cloned.1.call-done.corner_ref = f32[512,512]{1,0:T(8,128)} async-done(((f32[512,512]{1,0:T(8,128)}), f32[512,512]{1,0:T(8,128)}) %all-reduce.2.cloned.1.call-update) | async-done | bytes 1048592 | tf_op jit(solution)/shard_map/psum | solution.py:388
  190.1 0.0 copy-start
  190.1 1.4 copy-done
  191.5 0.0 copy-start.1
  191.5 1.2 copy-done.1
  192.7 71.8 %factor_and_solve.1 = f32[512,768]{1,0:T(8,128)S(1)} custom-call(f32[512,512]{1,0:T(8,128)S(1)} %copy-done.1, f32[512,768]{1,0:T(8,128)S(1)} %copy-done), custom_call_target="tpu_custom_call" | custom-call | tf_op jit(solution)/shard_map/factor_and_solve/pallas_call | solution.py:293
  264.5 0.5 copy.13
  265.0 1.3 collective-permute-start
  266.3 34.9 %collective-permute-done = f32[768,512]{1,0:T(8,128)} collective-permute-done((f32[768,512]{1,0:T(8,128)S(1)}, f32[768,512]{1,0:T(8,128)}, u32[]{:S(2)}, u32[]{:S(2)}) %collective-permute-start) | collective-permute-done | bytes 1572896 | tf_op jit(solution)/shard_map/ppermute | solution.py:393
  301.2 1.8 broadcast_select_fusion.across_ref
  302.9 0.0 copy-start.3
  303.0 0.1 constant_dynamic-slice_fusion
  303.0 1.5 collective-permute-start.1
  304.5 16.8 %collective-permute-done.1 = f32[384,512]{1,0:T(8,128)S(1)} collective-permute-done((f32[384,512]{1,0:T(8,128)S(1)}, f32[384,512]{1,0:T(8,128)S(1)}, u32[]{:S(2)}, u32[]{:S(2)}) %collective-permute-start.1) | collective-permute-done | bytes 786464 | tf_op jit(solution)/shard_map/ppermute | solution.py:409
  321.4 1.0 dynamic-slice_select_fusion
  322.4 0.0 all-gather.3.cloned.1.call-update
  322.4 0.0 copy-done.3
  322.4 850.1 %exchange.1 = (f32[4,4,4,1,1024,128]{5,4,3,2,1,0:T(8,128)}, f32[4,4,4,1,128,1024]{5,4,3,2,1,0:T(8,128)}) custom-call(f32[4096,2048]{1,0:T(8,128)} %bitcast.17, s32[1,64,64]{2,1,0:T(8,128)} %mask_ref.3), custom_call_target="tpu_custom_call" | custom-call | tf_op jit(solution)/shard_map/exchange/pallas_call | solution.py:185
  1172.6 0.7 pad_add_fusion.place_ref
  1173.3 0.0 all-gather.3.cloned.1.call-done
  1173.3 87.0 %assemble_schur.1 = (f32[6144,768]{1,0:T(8,128)}, f32[6144,512]{1,0:T(8,128)}) custom-call(s32[1152]{0:T(1024)} %copy-done.2, s32[2]{0:T(128)} %pad_add_fusion.place_ref, f32[6144,768]{1,0:T(8,128)} %parent_ref.3, f32[4,4,4,1,1024,128]{5,4,3,2,1,0:T(8,128)} %get-tuple-element.8.direct_ref, f32[4,4,4,1,128,1024]{5,4,3,2,1,0:T(8,128)} %get-tuple-element.9.turned_ref, ...), custom_call_target="tpu_custom_call" | custom-call | tf_op jit(solution)/shard_map/assemble_schur/pallas_call | solution.py:327
  (5 shorter events, 0.0 us)
Async XLA Ops:
  7.2 182.9 %all-reduce.2.cloned.1.call-start = ((), (), s32[]{:S(2)}) async-start(), calls=%async_computation | async-start | bytes 2097152 | tf_op jit(solution)/shard_map/psum | solution.py:388
  9.3 74.0 %copy-start.4 = (s32[4,64]{1,0:T(4,128)S(1)}, s32[4,64]{1,0:T(4,128)}, u32[]{:S(2)}) copy-start(s32[4,64]{1,0:T(4,128)} %param.6) | copy-start | bytes 3076
  84.8 10.4 copy-start.2
  96.4 1076.9 %all-gather.3.cloned.1.call-start = ((), (), s32[]{:S(2)}) async-start(), calls=%async_computation.1 | async-start | bytes 13369344 | tf_op jit(solution)/shard_map/all_gather | solution.py:411
  190.1 1.4 copy-start
  191.5 1.2 copy-start.1
  265.0 36.2 %collective-permute-start = (f32[768,512]{1,0:T(8,128)S(1)}, f32[768,512]{1,0:T(8,128)}, u32[]{:S(2)}, u32[]{:S(2)}) collective-permute-start(f32[768,512]{1,0:T(8,128)S(1)} %bitcast.20), channel_id=1, source_target_pairs={{0,4},{1,5},{2,6},{3,7},{8,12},{9,13},{10,14},{11,15},{16,20},{17,... | collective-permute-start | bytes 4718600 | tf_op jit(solution)/shard_map/ppermute | solution.py:393
  302.9 19.5 %copy-start.3 = (f32[768,512]{1,0:T(8,128)}, f32[768,512]{1,0:T(8,128)S(1)}, u32[]{:S(2)}) copy-start(f32[768,512]{1,0:T(8,128)S(1)} %broadcast_select_fusion.across_ref) | copy-start | bytes 4718596
  303.0 18.4 %collective-permute-start.1 = (f32[384,512]{1,0:T(8,128)S(1)}, f32[384,512]{1,0:T(8,128)S(1)}, u32[]{:S(2)}, u32[]{:S(2)}) collective-permute-start(f32[384,512]{1,0:T(8,128)S(1)} %constant_dynamic-slice_fusion), channel_id=1, source_target_pairs={{0,16},{1,17},{2,18},{3,19},{8,24},{9,25},{10,26},{11,27},{20,4},{... | collective-permute-start | bytes 2359304 | tf_op jit(solution)/shard_map/ppermute | solution.py:409
Sparse Core Ops, SparseCore 0:
  96.5 93.5 all-reduce.1
  322.5 249.7 all-gather.2
